TPU v7x, 32 devices: a whole 2x2x4 slice. The times are simulated.
32 devices in a mesh: groups: 2 (over x), seq: 16 (over z, y, core).
Axes of the slice: x: 2, y: 2, z: 4, core: 2. Of those that a mesh axis runs over, the one named last changes fastest.
Arguments:
- features: bfloat16 [4096, 2048], P(('groups', 'seq')), parts along dimension 0, may hold values from -40 to 40
- state_write: bfloat16 [4096, 64], P(('groups', 'seq')), parts along dimension 0, may hold values from -0.75 to 0.75
- state_read: bfloat16 [4096, 64], P(('groups', 'seq')), parts along dimension 0, may hold values from -0.75 to 0.75
- log_decay: float32 [4096, 32], P(('groups', 'seq')), parts along dimension 0, may hold values from -2 to 0
- skip_gain: float32 [32], replicated, may hold values from 1 to 4
- post_gain: float32 [2048], replicated, may hold values from 0.5 to 2
- start_index: int32 [4096], P(('groups', 'seq')), parts along dimension 0, may hold values from 0 to 2047, as said below
- step_noise: bfloat16 [3, 4096, 1024], P(None, ('groups', 'seq')), parts along dimension 1, may hold values from -4 to 4
- act_weight: bfloat16 [2048, 128], replicated, may hold values from -0.125 to 0.125
- dyn_weight: bfloat16 [2048, 1024], replicated, may hold values from -0.125 to 0.125
- act_in_weight: bfloat16 [128, 1024], replicated, may hold values from -0.5 to 0.5
- out_weight: bfloat16 [1024, 2048], replicated, may hold values from -0.1875 to 0.1875
- value_weight: bfloat16 [1024], replicated, may hold values from -0.1875 to 0.1875
Outputs:
- posterior: bfloat16 [4096, 2048], P(('groups', 'seq')), parts along dimension 0
- values: float32 [3, 4096], P(None, ('groups', 'seq')), parts along dimension 1
- final_latent: bfloat16 [4096, 2048], P(('groups', 'seq')), parts along dimension 0
There are 2 independent parts, one for each index of `groups`. A program takes and returns all parts, laid end to end along the dimension named above; an argument that names none is the same for every part. Nothing has to cross between parts.
Inputs may be any that keep to these rules, and one draw needn't show every extreme that they name: `start_index`: each aligned block of 128 starts (the starts of one device) names exactly 8 time steps in every aligned range of 128 time steps.
All inputs are finite; a program needn't handle non-finite values.
Results may differ from a plain program's by a relative error of at most 0.01.
Values may be sent and summed in bfloat16 or wider, within the bound.
A program may use at most 192 MiB of HBM per device.

v0:
```python
import functools
import jax
import jax.numpy as jnp
from jax import lax
from jax.experimental import pallas as pl
from jax.experimental.pallas import tpu as pltpu
from jax.sharding import PartitionSpec as P

F32 = jnp.float32
BF16 = jnp.bfloat16
VMEM_LIMIT = 56 * 1024 * 1024


def dot(a, b):
    return jnp.dot(a, b, preferred_element_type=F32)


def dot_nt(a, b):
    return lax.dot_general(a, b, (((1,), (1,)), ((), ())), preferred_element_type=F32)


def iota(shape, dim):
    return lax.broadcasted_iota(jnp.int32, shape, dim)


def plan(n, rows, width, state, starts):
    half = n // 2
    lanes = max(128, width // half)
    lane_blocks = width // lanes
    cuts = min(state // 16, half // lane_blocks)
    assert lane_blocks * cuts == half
    cap = starts // n
    pieces = max(1, 16 // cap)
    parts = 2 if width // 2 // pieces >= 128 and lane_blocks % 2 == 0 else 1
    return lanes, lane_blocks, cuts, cap, pieces, parts


def kernel(
    n,
    x_ref,
    write_ref,
    read_ref,
    decay_ref,
    skip_ref,
    gain_ref,
    start_ref,
    value_w_ref,
    noise_hbm,
    act_hbm,
    dyn_hbm,
    act_in_hbm,
    out_hbm,
    post,
    values_ref,
    latent,
    noise,
    act_w,
    dyn_w,
    act_in_w,
    out_w,
    meta_out,
    meta_in,
    end_out,
    end_in,
    carry_out,
    carry_in,
    cross_out,
    cross_in,
    local,
    entered,
    pick_out,
    pick_in,
    load_sem,
    meta_s,
    meta_r,
    end_s,
    end_r,
    carry_s,
    carry_r,
    cross_sem,
    pick_s,
    pick_r,
):
    rows, width = x_ref.shape
    heads = decay_ref.shape[0]
    state = write_ref.shape[0]
    starts = start_ref.shape[1]
    lanes, lane_blocks, cuts, cap, pieces, parts = plan(n, rows, width, state, starts)
    head_width = width // heads
    half = n // 2
    depth = state // cuts
    slot_rows = pieces * cap
    part_width = width // parts
    piece_width = part_width // pieces
    me = lax.axis_index("seq")
    upper = me // half
    mine = lax.rem(me, half)
    base_of_half = upper * half

    def far_first(i):
        step = n // 2 + (i + 1) // 2 * (2 * lax.rem(i, 2) - 1)
        return lax.rem(me + step, n)

    loads = [
        pltpu.make_async_copy(src, dst, load_sem.at[i])
        for i, (src, dst) in enumerate(
            (
                (act_hbm, act_w),
                (dyn_hbm, dyn_w),
                (act_in_hbm, act_in_w),
                (out_hbm, out_w),
                (noise_hbm, noise),
            )
        )
    ]
    for load in loads:
        load.start()

    barrier = pltpu.get_barrier_semaphore()

    def greet(j, _):
        pl.semaphore_signal(
            barrier,
            inc=1,
            device_id={"seq": lax.rem(me + j, n)},
            device_id_type=pl.DeviceIdType.MESH,
        )
        return 0

    lax.fori_loop(1, n, greet, 0)

    def remote(src, dst, send, recv, peer, slot):
        return pltpu.make_async_remote_copy(
            src_ref=src,
            dst_ref=dst,
            send_sem=send.at[peer],
            recv_sem=recv.at[slot],
            device_id={"seq": peer},
            device_id_type=pl.DeviceIdType.MESH,
        )

    lower = iota((rows, rows), 0) >= iota((rows, rows), 1)
    running_t = jnp.dot(
        decay_ref[...],
        (iota((rows, rows), 0) <= iota((rows, rows), 1)).astype(F32),
        precision=lax.Precision.HIGHEST,
        preferred_element_type=F32,
    )
    running = running_t.T
    spread = (
        iota((2 * heads, width), 1) // head_width == lax.rem(iota((2 * heads, width), 0), heads)
    ).astype(BF16)

    def widen(v):
        high = v.astype(BF16).astype(F32)
        return dot(jnp.concatenate([high, v - high], axis=1).astype(BF16), spread)

    x_all = x_ref[...].astype(F32)
    tail = widen(jnp.exp(running[rows - 1 : rows] - running))
    end_state = dot(write_ref[...], (x_all * tail).astype(BF16))
    whole_decay = widen(jnp.exp(running[rows - 8 : rows]))[7:8]
    start_row = start_ref[...].astype(F32)
    for k in range(half):
        at = slice((k // cuts) * lanes, (k // cuts + 1) * lanes)
        end_out[k] = end_state[(k % cuts) * depth : (k % cuts + 1) * depth, at].astype(BF16)
    decay_rows = lanes // 128
    for k in range(n):
        first_lane = (k % half) // cuts * lanes
        meta_out[k, 0:1, :] = start_row
        for i in range(decay_rows):
            lane = first_lane + i * 128
            meta_out[k, 1 + i : 2 + i, :] = whole_decay[:, lane : lane + 128]

    pl.semaphore_wait(barrier, n - 1)

    def send_end(j, _):
        k = lax.rem(mine + j, half)
        pltpu.make_async_remote_copy(
            src_ref=end_out.at[k],
            dst_ref=end_in.at[mine],
            send_sem=end_s.at[k],
            recv_sem=end_r.at[mine],
            device_id={"seq": base_of_half + k},
            device_id_type=pl.DeviceIdType.MESH,
        ).start()
        return 0

    lax.fori_loop(1, half, send_end, 0)

    def send_meta(i, _):
        peer = far_first(i)
        remote(meta_out.at[peer], meta_in.at[me], meta_s, meta_r, peer, me).start()
        return 0

    lax.fori_loop(0, n - 1, send_meta, 0)
    meta_in[pl.ds(me, 1)] = meta_out[pl.ds(me, 1)]
    end_in[pl.ds(mine, 1)] = end_out[pl.ds(mine, 1)]

    eye_rows = (iota((rows, rows), 0) == iota((rows, rows), 1)).astype(BF16)
    read = dot_nt(eye_rows, read_ref[...]).astype(BF16)
    gram = dot(read, write_ref[...])
    skip = widen(jnp.broadcast_to(skip_ref[...], (8, heads)))[0:1]
    per_tile = 128 // head_width
    head_of = iota((rows, 128), 1) // head_width

    def local_tiles(tiles):
        for tile in tiles:
            at = slice(tile * 128, (tile + 1) * 128)
            x_tile = x_ref[:, at].astype(F32)
            total = x_tile * skip[:, at]
            for inner in range(per_tile):
                h = tile * per_tile + inner
                gap = running[:, h : h + 1] - running_t[h : h + 1, :]
                weight = (jnp.exp(jnp.where(lower, gap, -jnp.inf)) * gram).astype(BF16)
                one_head = jnp.where(head_of == inner, x_tile, 0.0).astype(BF16)
                total = total + dot(weight, one_head)
            local[:, at] = total

    tiles = width // 128
    local_tiles(range(tiles // 2))

    def wait_meta(d):
        remote(meta_out.at[0], meta_in.at[d], meta_s, meta_r, d, d).wait_recv()

    def ends_lap(j, _):
        k = lax.rem(mine + j, half)
        pltpu.make_async_remote_copy(
            src_ref=end_out.at[0],
            dst_ref=end_in.at[k],
            send_sem=end_s.at[k],
            recv_sem=end_r.at[k],
            device_id={"seq": base_of_half + k},
            device_id_type=pl.DeviceIdType.MESH,
        ).wait_recv()
        wait_meta(base_of_half + k)
        return 0

    lax.fori_loop(1, half, ends_lap, 0)

    across = pltpu.make_async_remote_copy(
        src_ref=cross_out,
        dst_ref=cross_in,
        send_sem=cross_sem.at[0],
        recv_sem=cross_sem.at[1],
        device_id={"seq": lax.rem(me + half, n)},
        device_id_type=pl.DeviceIdType.MESH,
    )

    @pl.when(upper == 0)
    def _():
        cross_in[...] = jnp.zeros_like(cross_in)

    @pl.when(upper == 1)
    def _():
        across.wait_recv()

    def fold(d, carry):
        carry_out[d] = carry.astype(BF16)
        decay = jnp.concatenate(
            [meta_in[base_of_half + d, 1 + i : 2 + i, :] for i in range(decay_rows)], axis=1
        )
        return carry * decay + end_in[d].astype(F32)

    cross_out[...] = lax.fori_loop(0, half, fold, cross_in[...].astype(F32)).astype(BF16)

    @pl.when(upper == 0)
    def _():
        across.start()

    def send_carry(j, _):
        k = lax.rem(mine + j, half)
        pltpu.make_async_remote_copy(
            src_ref=carry_out.at[k],
            dst_ref=carry_in.at[mine],
            send_sem=carry_s.at[k],
            recv_sem=carry_r.at[mine],
            device_id={"seq": base_of_half + k},
            device_id_type=pl.DeviceIdType.MESH,
        ).start()
        return 0

    lax.fori_loop(1, half, send_carry, 0)
    carry_in[pl.ds(mine, 1)] = carry_out[pl.ds(mine, 1)]

    local_tiles(range(tiles // 2, tiles))
    entered[...] = widen(jnp.exp(running))

    def metas_lap(j, _):
        wait_meta(lax.rem(base_of_half + half + j, n))
        return 0

    lax.fori_loop(0, half, metas_lap, 0)

    asked = meta_in[:, 0, :starts]
    base = (me * rows).astype(F32)
    hit = jnp.logical_and(asked >= base, asked < base + rows)
    up_to = (iota((starts, starts), 0) <= iota((starts, starts), 1)).astype(BF16)
    rank = dot(hit.astype(F32).astype(BF16), up_to)
    rank = jnp.where(hit, rank, 0.0).astype(BF16)
    offset = jnp.where(hit, asked - base, 0.0).astype(BF16)
    slots = n * slot_rows
    repeat = (iota((slots, n), 0) // slot_rows == iota((slots, n), 1)).astype(BF16)
    slot_at = iota((slots, starts), 0)
    chosen = dot(repeat, rank) == (slot_at % cap + 1).astype(F32)
    wanted = jnp.sum(jnp.where(chosen, dot(repeat, offset), 0.0), axis=1, keepdims=True)
    row_at = iota((slots, rows), 0)
    picks_row = wanted == iota((slots, rows), 1).astype(F32)
    picks = [
        jnp.where(jnp.logical_and(picks_row, (row_at // cap) % pieces == p), 1.0, 0.0).astype(BF16)
        for p in range(pieces)
    ]

    start_col = jnp.sum(
        jnp.where(iota((starts, starts), 0) == iota((starts, starts), 1), start_row, 0.0),
        axis=1,
        keepdims=True,
    )
    first = (iota((starts, n), 1) * rows).astype(F32)
    from_owner = jnp.logical_and(start_col >= first, start_col < first + rows)
    before = (iota((starts, starts), 0) >= iota((starts, starts), 1)).astype(BF16)
    count = dot(before, from_owner.astype(F32).astype(BF16))
    lands = jnp.sum(
        jnp.where(from_owner, count - 1.0 + (iota((starts, n), 1) * slot_rows).astype(F32), 0.0),
        axis=1,
        keepdims=True,
    )

    def carry_lap(k, _):
        @pl.when(k != mine)
        def _():
            pltpu.make_async_remote_copy(
                src_ref=carry_out.at[0],
                dst_ref=carry_in.at[k],
                send_sem=carry_s.at[k],
                recv_sem=carry_r.at[k],
                device_id={"seq": base_of_half + k},
                device_id_type=pl.DeviceIdType.MESH,
            ).wait_recv()

        return 0

    same_head = jnp.where(
        iota((lanes, lanes), 0) // head_width == iota((lanes, lanes), 1) // head_width,
        1.0 / head_width,
        0.0,
    ).astype(BF16)
    for part in range(parts):
        lax.fori_loop(part * half // parts, (part + 1) * half // parts, carry_lap, 0)
        for block in range(part * lane_blocks // parts, (part + 1) * lane_blocks // parts):
            at = slice(block * lanes, (block + 1) * lanes)
            carry = carry_in[block * cuts : (block + 1) * cuts].reshape(state, lanes)
            mixed = local[:, at] + dot(read, carry) * entered[:, at]
            square_mean = dot((mixed * mixed).astype(BF16), same_head)
            post[:, at] = (mixed * lax.rsqrt(square_mean + 1e-05) * gain_ref[:, at]).astype(BF16)
        picked = 0.0
        for p in range(pieces):
            lane = part * part_width + p * piece_width
            picked = picked + dot(picks[p], post[:, lane : lane + piece_width])
        pick_out[part] = picked.astype(BF16).reshape(n, slot_rows, piece_width)

        def send_rows(i, _):
            peer = far_first(i)
            remote(
                pick_out.at[part, peer],
                pick_in.at[part, me],
                pick_s.at[part],
                pick_r.at[part],
                peer,
                me,
            ).start()
            return 0

        lax.fori_loop(0, n - 1, send_rows, 0)
        pick_in[part, pl.ds(me, 1)] = pick_out[part, pl.ds(me, 1)]
    for load in loads:
        load.wait()

    slot_of = iota((starts, slots), 1).astype(F32)
    act_sum, dyn_sum = 0.0, 0.0
    for part in range(parts):

        def row_lap(j, _):
            peer = lax.rem(me + j, n)
            remote(
                pick_out.at[part, 0],
                pick_in.at[part, peer],
                pick_s.at[part],
                pick_r.at[part],
                peer,
                peer,
            ).wait_recv()
            return 0

        lax.fori_loop(1, n, row_lap, 0)
        landed = pick_in[part].reshape(slots, piece_width)
        for p in range(pieces):
            place = jnp.where(slot_of == lands + float(p * cap), 1.0, 0.0).astype(BF16)
            lane = part * part_width + p * piece_width
            latent[:, lane : lane + piece_width] = dot(place, landed).astype(BF16)
        at = slice(part * part_width, (part + 1) * part_width)
        act_sum = act_sum + dot(latent[:, at], act_w[at, :])
        dyn_sum = dyn_sum + dot(latent[:, at], dyn_w[at, :])

    diagonal = iota((starts, starts), 0) == iota((starts, starts), 1)
    value_rows = value_w_ref[...].astype(F32)
    value_w = jnp.concatenate(
        [value_rows[i : i + 1] for i in range(value_rows.shape[0])], axis=1
    )
    for step in range(noise.shape[0]):
        wide = latent[...].astype(F32)
        scale = lax.rsqrt(jnp.mean(wide * wide, axis=-1, keepdims=True) + 1e-06)
        if step > 0:
            act_sum = dot(latent[...], act_w[...])
            dyn_sum = dot(latent[...], dyn_w[...])
        action = jnp.tanh(act_sum * scale).astype(BF16)
        inner = dyn_sum * scale + dot(action, act_in_w[...])
        hidden = (inner / (1.0 + jnp.exp(-inner)) + noise[step].astype(F32)).astype(BF16)
        value = jnp.sum(hidden.astype(F32) * value_w, axis=1, keepdims=True)
        values_ref[step : step + 1, :] = jnp.sum(
            jnp.where(diagonal, value, 0.0), axis=0, keepdims=True
        )
        latent[...] = (wide + dot(hidden, out_w[...])).astype(BF16)

    def sent(j, _):
        peer = lax.rem(me + j, n)
        remote(meta_out.at[0], meta_in.at[me], meta_s, meta_r, peer, me).wait_send()
        for part in range(parts):
            remote(
                pick_out.at[part, 0],
                pick_in.at[part, me],
                pick_s.at[part],
                pick_r.at[part],
                peer,
                me,
            ).wait_send()

        return 0

    lax.fori_loop(1, n, sent, 0)

    def sent_in_half(j, _):
        k = lax.rem(mine + j, half)
        for src, dst, send, recv in (
            (end_out, end_in, end_s, end_r),
            (carry_out, carry_in, carry_s, carry_r),
        ):
            pltpu.make_async_remote_copy(
                src_ref=src.at[0],
                dst_ref=dst.at[mine],
                send_sem=send.at[k],
                recv_sem=recv.at[mine],
                device_id={"seq": base_of_half + k},
                device_id_type=pl.DeviceIdType.MESH,
            ).wait_send()
        return 0

    lax.fori_loop(1, half, sent_in_half, 0)

    @pl.when(upper == 0)
    def _():
        across.wait_send()


def hand_over(*refs):
    sem = refs[6]
    copies = [pltpu.make_async_copy(refs[i], refs[3 + i], sem.at[i]) for i in range(3)]
    for copy in copies:
        copy.start()
    for copy in copies:
        copy.wait()


def per_device(
    features,
    state_write,
    state_read,
    log_decay,
    skip_gain,
    post_gain,
    start_index,
    step_noise,
    act_weight,
    dyn_weight,
    act_in_weight,
    out_weight,
    value_weight,
):
    n = lax.axis_size("seq")
    rows, width = features.shape
    state = state_write.shape[1]
    starts = start_index.shape[0]
    lanes, lane_blocks, cuts, cap, pieces, parts = plan(n, rows, width, state, starts)
    half, depth, slot_rows = n // 2, state // cuts, pieces * cap
    vmem = pl.BlockSpec(memory_space=pltpu.VMEM)
    hbm = pl.BlockSpec(memory_space=pl.ANY)
    sems = pltpu.SemaphoreType.DMA((n,))
    half_sems = pltpu.SemaphoreType.DMA((half,))
    flops = 2 * step_noise.shape[0] * starts * (dyn_weight.size + out_weight.size)
    results = pl.pallas_call(
        functools.partial(kernel, n),
        out_shape=(
            pltpu.VMEM((rows, width), BF16),
            pltpu.VMEM((step_noise.shape[0], starts), F32),
            pltpu.VMEM((starts, width), BF16),
        ),
        in_specs=[vmem] * 8 + [hbm] * 5,
        out_specs=(vmem, vmem, vmem),
        scratch_shapes=[
            pltpu.VMEM(step_noise.shape, BF16),
            pltpu.VMEM(act_weight.shape, BF16),
            pltpu.VMEM(dyn_weight.shape, BF16),
            pltpu.VMEM(act_in_weight.shape, BF16),
            pltpu.VMEM(out_weight.shape, BF16),
            pltpu.VMEM((n, 8, 128), F32),
            pltpu.VMEM((n, 8, 128), F32),
            pltpu.VMEM((half, depth, lanes), BF16),
            pltpu.VMEM((half, depth, lanes), BF16),
            pltpu.VMEM((half, depth, lanes), BF16),
            pltpu.VMEM((half, depth, lanes), BF16),
            pltpu.VMEM((depth, lanes), BF16),
            pltpu.VMEM((depth, lanes), BF16),
            pltpu.VMEM((rows, width), F32),
            pltpu.VMEM((rows, width), F32),
            pltpu.VMEM((parts, n, slot_rows, width // parts // pieces), BF16),
            pltpu.VMEM((parts, n, slot_rows, width // parts // pieces), BF16),
            pltpu.SemaphoreType.DMA((5,)),
            sems,
            sems,
            half_sems,
            half_sems,
            half_sems,
            half_sems,
            pltpu.SemaphoreType.DMA((2,)),
            pltpu.SemaphoreType.DMA((parts, n)),
            pltpu.SemaphoreType.DMA((parts, n)),
        ],
        compiler_params=pltpu.CompilerParams(
            collective_id=0, has_side_effects=True, vmem_limit_bytes=VMEM_LIMIT
        ),
        cost_estimate=pl.CostEstimate(
            flops=flops, bytes_accessed=12 * 1024 * 1024, transcendentals=1024 * 1024
        ),
    )(
        features,
        state_write.T,
        state_read.T,
        log_decay.T,
        skip_gain[None, :],
        post_gain[None, :],
        start_index[None, :],
        value_weight.reshape(-1, 128),
        step_noise,
        act_weight,
        dyn_weight,
        act_in_weight,
        out_weight,
    )
    return pl.pallas_call(
        hand_over,
        out_shape=tuple(jax.ShapeDtypeStruct(r.shape, r.dtype) for r in results),
        in_specs=[vmem] * 3,
        out_specs=(hbm, hbm, hbm),
        scratch_shapes=[pltpu.SemaphoreType.DMA((3,))],
    )(*results)


def solution(mesh):
    split = P(("groups", "seq"), None)
    placed = (
        split,
        split,
        split,
        split,
        P(),
        P(),
        P(("groups", "seq")),
        P(None, ("groups", "seq"), None),
        P(),
        P(),
        P(),
        P(),
        P(),
    )
    return jax.shard_map(
        per_device,
        mesh=mesh,
        in_specs=placed,
        out_specs=(split, P(None, ("groups", "seq")), split),
        check_vma=False,
    )
```

profile of v0, /device:TPU:0, one launch (start us, length us, event | category | flops | bytes accessed | tf_op | source)
XLA Modules:
  0.0 45.1 jit_solution(14345463372308793906)
XLA Ops:
  0.6 40.1 %shard_map.148 = (bf16[128,2048]{1,0:T(8,128)(2,1)S(1)}, f32[3,128]{1,0:T(4,128)S(1)}, bf16[128,2048]{1,0:T(8,128)(2,1)S(1)}) custom-call(bf16[128,2048]{1,0:T(8,128)(2,1)} %x_ref.1, bf16[64,128]{1,0:T(8,128)(2,1)} %bitcast.7, bf16[64,128]{1,0:T(8,128)(2,1)} %bitcast.8, f32[32,128]{1,0:T(8,128)} %bitcast.9, f32[1,32]{1,0:T(1,128)} %bitcast.12, ...), custom_call_target="tpu_custom_call" | custom-call | flops 3221225472 | bytes 12582912 | tf_op jit(solution)/shard_map/pallas_call | solution.py:499
  40.7 0.0 copy-start
  40.7 0.8 %copy-done = bf16[128,2048]{1,0:T(8,128)(2,1)} copy-done((bf16[128,2048]{1,0:T(8,128)(2,1)}, bf16[128,2048]{1,0:T(8,128)(2,1)S(1)}, u32[]{:S(2)}) %copy-start) | copy-done | bytes 524312
  41.5 0.0 copy-start.1
  41.5 0.8 %copy-done.1 = bf16[128,2048]{1,0:T(8,128)(2,1)} copy-done((bf16[128,2048]{1,0:T(8,128)(2,1)}, bf16[128,2048]{1,0:T(8,128)(2,1)S(1)}, u32[]{:S(2)}) %copy-start.1) | copy-done | bytes 524312
  42.3 0.0 copy-start.2
  42.3 0.6 %copy-done.2 = f32[3,128]{1,0:T(4,128)} copy-done((f32[3,128]{1,0:T(4,128)}, f32[3,128]{1,0:T(4,128)S(1)}, u32[]{:S(2)}) %copy-start.2) | copy-done | bytes 1560
  42.9 2.2 %shard_map.149 = (bf16[128,2048]{1,0:T(8,128)(2,1)}, f32[3,128]{1,0:T(4,128)}, bf16[128,2048]{1,0:T(8,128)(2,1)}) custom-call(bf16[128,2048]{1,0:T(8,128)(2,1)} %copy-done, f32[3,128]{1,0:T(4,128)} %copy-done.2, bf16[128,2048]{1,0:T(8,128)(2,1)} %copy-done.1), custom_call_target="tpu_custom_call" | custom-call | tf_op jit(solution)/shard_map/pallas_call | solution.py:558
Async XLA Ops:
  40.7 0.8 %copy-start = (bf16[128,2048]{1,0:T(8,128)(2,1)}, bf16[128,2048]{1,0:T(8,128)(2,1)S(1)}, u32[]{:S(2)}) copy-start(bf16[128,2048]{1,0:T(8,128)(2,1)S(1)} %get-tuple-element.6.refs_0_) | copy-start | bytes 1572868
  41.5 0.8 %copy-start.1 = (bf16[128,2048]{1,0:T(8,128)(2,1)}, bf16[128,2048]{1,0:T(8,128)(2,1)S(1)}, u32[]{:S(2)}) copy-start(bf16[128,2048]{1,0:T(8,128)(2,1)S(1)} %get-tuple-element.8.refs_2_) | copy-start | bytes 1572868
  42.3 0.6 %copy-start.2 = (f32[3,128]{1,0:T(4,128)}, f32[3,128]{1,0:T(4,128)S(1)}, u32[]{:S(2)}) copy-start(f32[3,128]{1,0:T(4,128)S(1)} %get-tuple-element.7.refs_1_) | copy-start | bytes 4612
where the time goes:
time: 45.2 us; the launch traced here: 45.1 us
  Pallas kernels  42.3 us (94%)
  local copies, waits for them, and re-layouts  2.15 us (5%)
  between operations  0.65 us (1%)
    pallas_call x1, Pallas kernels, per_device(): pl.pallas_call(functools.partial(kernel, n), out_shape=(pltpu.VMEM((rows,...  40.1 us
    pallas_call x1, Pallas kernels, per_device(): pl.pallas_call(hand_over, out_shape=tuple((jax.ShapeDtypeStruct(r.shape,...  2.2 us
    unnamed x6, local copies, waits for them, and re-layouts  2.15 us

commit v1 on v0

--- a/solution.py
+++ b/solution.py
@@ -561,6 +561,7 @@
         in_specs=[vmem] * 3,
         out_specs=(hbm, hbm, hbm),
         scratch_shapes=[pltpu.SemaphoreType.DMA((3,))],
+        compiler_params=pltpu.CompilerParams(vmem_limit_bytes=VMEM_LIMIT // 7),
     )(*results)
 
 

time: 45.2 us -> 41.9 us (0.927)
  local copies, waits for them, and re-layouts: 2.15 us -> 0 us
  Pallas kernels: 42.3 us -> 41.1 us
    unnamed x6 -> x0, local copies, waits for them, and re-layouts: 2.15 us -> none
    pallas_call x1, Pallas kernels: 2.2 us -> 1 us  [per_device(): pl.pallas_call(hand_over, out_shape=tuple((jax.ShapeDtypeStruct(r.shape,...]
where the time goes in v1:
time: 41.9 us; the launch traced here: 41.7 us
  Pallas kernels  41.1 us (98%)
  between operations  0.64 us (2%)
    pallas_call x1, Pallas kernels, per_device(): pl.pallas_call(functools.partial(kernel, n), out_shape=(pltpu.VMEM((rows,...  40.1 us
    pallas_call x1, Pallas kernels, per_device(): pl.pallas_call(hand_over, out_shape=tuple((jax.ShapeDtypeStruct(r.shape,...  1 us

profile of v1, /device:TPU:0, one launch (start us, length us, event | category | flops | bytes accessed | tf_op | source)
XLA Modules:
  0.0 41.7 jit_solution(13772039727597581064)
XLA Ops:
  0.6 40.1 %shard_map.148 = (bf16[128,2048]{1,0:T(8,128)(2,1)S(1)}, f32[3,128]{1,0:T(4,128)S(1)}, bf16[128,2048]{1,0:T(8,128)(2,1)S(1)}) custom-call(bf16[128,2048]{1,0:T(8,128)(2,1)} %x_ref.1, bf16[64,128]{1,0:T(8,128)(2,1)} %bitcast.7, bf16[64,128]{1,0:T(8,128)(2,1)} %bitcast.8, f32[32,128]{1,0:T(8,128)} %bitcast.9, f32[1,32]{1,0:T(1,128)} %bitcast.12, ...), custom_call_target="tpu_custom_call" | custom-call | flops 3221225472 | bytes 12582912 | tf_op jit(solution)/shard_map/pallas_call | solution.py:499
  40.7 1.0 %shard_map.149 = (bf16[128,2048]{1,0:T(8,128)(2,1)}, f32[3,128]{1,0:T(4,128)}, bf16[128,2048]{1,0:T(8,128)(2,1)}) custom-call(bf16[128,2048]{1,0:T(8,128)(2,1)S(1)} %get-tuple-element.6.refs_0_, f32[3,128]{1,0:T(4,128)S(1)} %get-tuple-element.7.refs_1_, bf16[128,2048]{1,0:T(8,128)(2,1)S(1)} %get-tuple-element.8.refs_2_), custom_call_target="tpu_custom_call" | custom-call | tf_op jit(solution)/shard_map/pallas_call | solution.py:558
